TPU v7x, 256 devices: a whole 4x4x8 slice. The times are simulated.
256 devices in a mesh: chan: 32 (over y_lo, z, core), seq: 8 (over y_hi, x).
Axes of the slice: x: 4, y: 4 (y_hi: 2, y_lo: 2; y = y_hi * 2 + y_lo), z: 8, core: 2. Of those that a mesh axis runs over, the one named last changes fastest.
Arguments:
- query_input: bfloat16 [8192, 8192], P('seq', 'chan'), may hold values from -6 to 6
- key_input: bfloat16 [8192, 8192], P('seq', 'chan'), may hold values from -6 to 6
- value_input: bfloat16 [8192, 8192], P('seq', 'chan'), may hold values from -6 to 6
- filter_spectrum: bfloat16 [1024, 16, 2, 8192], P('seq', None, None, 'chan'), may hold values from -6 to 6
- out_weight: bfloat16 [8192, 8192], P('chan'), may hold values from -0.125 to 0.125
Outputs:
- mixed: bfloat16 [8192, 8192], P('chan', 'seq')
All inputs are finite; a program needn't handle non-finite values.
Results may differ from a plain program's by a relative error of at most 0.03.
Values may be sent and summed in bfloat16 or wider, within the bound.
A program may use at most 128 MiB of HBM per device.

v0:
```python
import functools
import math

import jax
import jax.numpy as jnp
import ml_dtypes
import numpy as np
from jax import lax
from jax.experimental import pallas as pl
from jax.experimental.pallas import tpu as pltpu
from jax.sharding import PartitionSpec as P

BF = jnp.bfloat16
F32 = jnp.float32
ORDER = 1024
SHORT = 16
TOTAL = ORDER * SHORT
SEQ = 8
SUB = 32
LANES = SHORT * SUB
MESH = pl.DeviceIdType.MESH
QUARTER = 256
ORDER_OF_QUARTERS = (0, 2, 1, 3)


def make_tables():
    step = np.arange(ORDER)
    angle = 2.0 * math.pi / ORDER * (np.outer(step, step) % ORDER)
    long_cos = np.cos(angle)
    long_nsin = -np.sin(angle)
    short = np.arange(SHORT)
    angle = 2.0 * math.pi / SHORT * (np.outer(short, short) % SHORT)
    eye = np.eye(SUB)
    short_cos = np.kron(np.cos(angle), eye)
    short_sin = np.kron(np.sin(angle), eye)
    forth = np.block([[short_cos, -short_sin], [short_sin, short_cos]])
    back = np.block([[short_cos, short_sin], [-short_sin, short_cos]])
    angle = 2.0 * math.pi / TOTAL * np.outer(step, short)
    twist_cos = np.repeat(np.cos(angle), SUB, axis=1)
    twist_sin = np.repeat(np.sin(angle), SUB, axis=1)
    rows = np.zeros((512, 512))
    first, second = np.meshgrid(np.arange(32), np.arange(16), indexing="ij")
    rows[(second * 32 + first).ravel(), (first * 16 + second).ravel()] = 1.0
    lanes = np.zeros((512, 512))
    outer, inner, chan = np.meshgrid(np.arange(4), np.arange(4), np.arange(32), indexing="ij")
    lanes[
        (outer * 128 + inner * 32 + chan).ravel(), (inner * 128 + outer * 32 + chan).ravel()
    ] = 1.0

    def half(array):
        return array.astype(np.float32).astype(ml_dtypes.bfloat16)

    return (
        half(np.stack([rows, rows.T, lanes])),
        half(np.stack([long_cos, long_nsin])),
        np.stack([twist_cos, twist_sin]).astype(np.float32),
        half(np.stack([forth, back])),
    )


def dot(left, right):
    return jnp.dot(left, right, preferred_element_type=F32)


def arrive(ref, sem):
    pltpu.make_async_copy(ref, ref, sem).wait()


def kernel(
    query,
    key,
    value,
    filt,
    weight,
    moves,
    long_table,
    twist,
    short_table,
    out,
    query_v,
    key_v,
    value_v,
    filt_v,
    moves_v,
    long_v,
    twist_v,
    short_v,
    sorted_v,
    prod_send,
    prod_recv,
    filt_send,
    filt_recv,
    field,
    total,
    conv_send,
    conv_recv,
    gated,
    weights,
    ring_send,
    ring_recv,
    local_sem,
    prod_ss,
    prod_rs,
    filt_ss,
    filt_rs,
    conv_ss,
    conv_rs,
    weight_ss,
    weight_rs,
    gate_ss,
    gate_rs,
    ring_ss,
    ring_rs,
):
    chan = lax.axis_index("chan")
    me = lax.axis_index("seq")
    y_lo, z, core = chan // 16, (chan // 2) % 8, chan % 2
    y_hi, x = me // 4, me % 4

    def chan_of(low, depth, which):
        return (low * 8 + depth) * 2 + which

    sibling = {"chan": chan_of(y_lo, z, 1 - core), "seq": me}
    across = {"chan": chan_of(1 - y_lo, z, core), "seq": me}
    far = (1 - y_hi) * 4 + x
    z_up = (z + 1) % 8
    z_down = (z + 7) % 8
    up = {"chan": chan_of(y_lo, z_up, core), "seq": me}
    down = {"chan": chan_of(y_lo, z_down, core), "seq": me}

    local = [
        (key, key_v),
        (value, value_v),
        (moves, moves_v),
        (filt, filt_v),
        (long_table, long_v),
        (twist, twist_v),
        (short_table, short_v),
        (query, query_v),
    ]
    for at, (source, target) in enumerate(local):
        pltpu.make_async_copy(source, target, local_sem.at[at]).start()

    def local_done(at):
        pltpu.make_async_copy(local[at][0], local[at][1], local_sem.at[at]).wait()

    barrier = pltpu.get_barrier_semaphore()

    def greet(step, carry):
        peer = (me + step) % SEQ
        pl.semaphore_signal(barrier, 1, device_id={"chan": chan, "seq": peer}, device_id_type=MESH)
        return carry

    lax.fori_loop(1, SEQ, greet, 0)
    for peer in (
        sibling,
        up,
        down,
        across,
        {"chan": chan_of(1 - y_lo, z, 1 - core), "seq": me},
        {"chan": chan_of(1 - y_lo, z, core), "seq": far},
        {"chan": chan_of(1 - y_lo, z, 1 - core), "seq": far},
    ):
        pl.semaphore_signal(barrier, 1, device_id=peer, device_id_type=MESH)

    local_done(0)
    local_done(1)
    local_done(2)
    for half in range(2):
        rows = pl.ds(half * 512, 512)
        product = (key_v[rows, :].astype(F32) * value_v[rows, :].astype(F32)).astype(BF)
        moved = dot(moves_v[0], product).astype(BF)
        sorted_v[:, pl.ds(half * 32, 32), :] = moved.reshape(SHORT, 32, 256)
    for tile in range(2):
        block = jnp.concatenate(
            [
                jnp.concatenate(
                    [sorted_v[4 * group + b, :, pl.ds(tile * 128, 128)] for b in range(4)], axis=1
                )
                for group in range(4)
            ],
            axis=0,
        )
        moved = dot(block, moves_v[2]).astype(BF)
        for owner in range(4):
            for group in range(4):
                prod_send[4 * tile + owner, :, pl.ds(group * 128, 128)] = moved[
                    group * 64 : (group + 1) * 64, owner * 128 : (owner + 1) * 128
                ]
    pl.semaphore_wait(barrier, SEQ - 1 + 7)

    def spread(send, recv, ss, rs):
        def one(step, carry):
            peer = (me + step) % SEQ
            pltpu.make_async_remote_copy(
                send.at[peer],
                recv.at[me],
                ss.at[peer],
                rs.at[me],
                device_id={"chan": chan, "seq": peer},
                device_id_type=MESH,
            ).start()
            return carry

        lax.fori_loop(1, SEQ, one, 0)
        pltpu.make_async_copy(send.at[me], recv.at[me], rs.at[me]).start()

    def spread_done(send, ss):
        def one(step, carry):
            peer = (me + step) % SEQ
            arrive(send.at[peer], ss.at[peer])
            return carry

        lax.fori_loop(1, SEQ, one, 0)

    spread(prod_send, prod_recv, prod_ss, prod_rs)

    local_done(3)

    def sort_filter(group, carry):
        for tile in range(2):
            block = jnp.concatenate(
                [
                    jnp.concatenate(
                        [filt_v[part, 4 * group + b, :, pl.ds(tile * 128, 128)] for b in range(4)],
                        axis=1,
                    )
                    for part in range(2)
                ],
                axis=0,
            )
            moved = dot(block, moves_v[2]).astype(BF)
            lanes = pl.ds(pl.multiple_of(group * 128, 128), 128)
            for owner in range(4):
                for part in range(2):
                    filt_send[4 * tile + owner, part, :, lanes] = moved[
                        part * 128 : (part + 1) * 128, owner * 128 : (owner + 1) * 128
                    ]
        return carry

    lax.fori_loop(0, 4, sort_filter, 0)
    spread(filt_send, filt_recv, filt_ss, filt_rs)

    def weight_block(low, depth, which):
        at = pl.multiple_of(chan_of(low, depth, which) * 256, 256)
        return weight.at[:, pl.ds(at, 256)]

    def send_weight(depth, carry):
        pltpu.make_async_copy(
            weight_block(y_lo, depth, core), weights.at[depth, pl.ds(0, 256), :], weight_rs.at[depth]
        ).start()
        pltpu.make_async_remote_copy(
            weight_block(y_lo, depth, 1 - core),
            weights.at[depth, pl.ds(256, 256), :],
            weight_ss,
            weight_rs.at[depth],
            device_id=sibling,
            device_id_type=MESH,
        ).start()
        seq_to = ((y_hi + depth) % 2) * 4 + x
        for slot, which in ((2, core), (3, 1 - core)):
            pltpu.make_async_remote_copy(
                weight_block(1 - y_lo, depth, which),
                weights.at[depth, pl.ds(slot * 256, 256), :],
                weight_ss,
                weight_rs.at[depth],
                device_id={"chan": chan_of(1 - y_lo, z, which), "seq": seq_to},
                device_id_type=MESH,
            ).start()
        return carry

    lax.fori_loop(0, 8, send_weight, 0)

    local_done(4)
    local_done(5)
    local_done(6)

    def wait_product(peer, carry):
        arrive(prod_recv.at[peer], prod_rs.at[peer])
        return carry

    lax.fori_loop(0, SEQ, wait_product, 0)

    def forward(step, carry):
        rows = pl.ds(pl.multiple_of(step * 256, 256), 256)
        values = prod_recv[...].reshape(512, LANES)
        real = dot(long_v[0, rows, pl.ds(0, 512)], values)
        imag = dot(long_v[1, rows, pl.ds(0, 512)], values)
        tw_cos = twist_v[0, rows, :]
        tw_sin = twist_v[1, rows, :]
        both = jnp.concatenate(
            [
                (real * tw_cos + imag * tw_sin).astype(BF),
                (imag * tw_cos - real * tw_sin).astype(BF),
            ],
            axis=1,
        )
        field[rows, :] = dot(both, short_v[0])
        return carry

    lax.fori_loop(0, 4, forward, 0)

    total[...] = jnp.zeros_like(total)

    def backward(step, carry):
        near = step % 4
        peer = ((y_hi + step // 4) % 2) * 4 + (x + near + near // 2 - 2 * (near // 3)) % 4
        arrive(filt_recv.at[peer], filt_rs.at[peer])
        rows = pl.ds(pl.multiple_of(peer * 128, 128), 128)
        real = field[rows, pl.ds(0, LANES)]
        imag = field[rows, pl.ds(LANES, LANES)]
        filt_real = filt_recv[peer, 0].astype(F32)
        filt_imag = filt_recv[peer, 1].astype(F32)
        both = jnp.concatenate(
            [
                (real * filt_real - imag * filt_imag).astype(BF),
                (real * filt_imag + imag * filt_real).astype(BF),
            ],
            axis=1,
        )
        mixed = dot(both, short_v[1])
        real = mixed[:, :LANES]
        imag = mixed[:, LANES:]
        tw_cos = twist_v[0, rows, :]
        tw_sin = twist_v[1, rows, :]
        turned = jnp.concatenate(
            [
                (real * tw_cos - imag * tw_sin).astype(BF),
                (imag * tw_cos + real * tw_sin).astype(BF),
            ],
            axis=0,
        )
        table = jnp.concatenate(
            [long_v[0, pl.ds(0, 512), rows], long_v[1, pl.ds(0, 512), rows]], axis=1
        )
        total[...] += dot(table, turned)
        return carry

    lax.fori_loop(0, SEQ, backward, 0)
    conv_send[...] = (total[...] * (1.0 / TOTAL)).astype(BF).reshape(SEQ, 64, LANES)
    spread(conv_send, conv_recv, conv_ss, conv_rs)

    local_done(7)

    def wait_conv(peer, carry):
        arrive(conv_recv.at[peer], conv_rs.at[peer])
        return carry

    lax.fori_loop(0, SEQ, wait_conv, 0)
    for tile in range(2):
        block = jnp.concatenate(
            [
                jnp.concatenate(
                    [conv_recv[4 * tile + owner, :, pl.ds(group * 128, 128)] for owner in range(4)],
                    axis=1,
                )
                for group in range(4)
            ],
            axis=0,
        )
        moved = dot(block, moves_v[2]).astype(BF)
        for group in range(4):
            for b in range(4):
                sorted_v[4 * group + b, :, pl.ds(tile * 128, 128)] = moved[
                    group * 64 : (group + 1) * 64, b * 128 : (b + 1) * 128
                ]
    for half in range(2):
        rows = pl.ds(half * 512, 512)
        block = sorted_v[:, pl.ds(half * 32, 32), :].reshape(512, 256)
        conv = dot(moves_v[1], block)
        gated[rows, pl.ds(0, 256)] = (query_v[rows, :].astype(F32) * conv).astype(BF)

    def part(quarter, slot):
        return gated.at[pl.ds(quarter * QUARTER, QUARTER), pl.ds(slot * 256, 256)]

    def gate_copy(kind, quarter, source, target, device):
        return pltpu.make_async_remote_copy(
            part(quarter, source),
            part(quarter, target),
            gate_ss.at[kind, quarter],
            gate_rs.at[kind, quarter],
            device_id=device,
            device_id_type=MESH,
        )

    for quarter in ORDER_OF_QUARTERS:
        gate_copy(0, quarter, 0, 2, across).start()
        gate_copy(1, quarter, 0, 1, sibling).start()

    def wait_weight(depth, carry):
        arrive(weights.at[depth], weight_rs.at[depth])
        return carry

    lax.fori_loop(0, 8, wait_weight, 0)

    def stream(quarter):
        return (quarter // 2, quarter % 2)

    def block_at(quarter, step):
        if quarter // 2 == 0:
            return (z + 15 - step) % 8
        return (z + 1 + step) % 8

    def term(quarter, step):
        rows = pl.ds(quarter * QUARTER, QUARTER)
        return dot(gated[rows, :], weights[block_at(quarter, step)])

    def ring_copy(quarter, step):
        way, sub = stream(quarter)
        return pltpu.make_async_remote_copy(
            ring_send.at[way, sub, step],
            ring_recv.at[way, sub, step],
            ring_ss.at[way, sub, step],
            ring_rs.at[way, sub, step],
            device_id=up if way == 0 else down,
            device_id_type=MESH,
        )

    for quarter in ORDER_OF_QUARTERS:
        way, sub = stream(quarter)
        arrive(part(quarter, 2), gate_rs.at[0, quarter])
        gate_copy(2, quarter, 2, 3, sibling).start()
        arrive(part(quarter, 1), gate_rs.at[1, quarter])
        arrive(part(quarter, 3), gate_rs.at[2, quarter])
        ring_send[way, sub, 0] = term(quarter, 0).astype(BF)
        ring_copy(quarter, 0).start()

    def ring_step(step, carry):
        for quarter in ORDER_OF_QUARTERS:
            way, sub = stream(quarter)
            own = term(quarter, step)
            ring_copy(quarter, step - 1).wait_recv()
            ring_send[way, sub, step] = (own + ring_recv[way, sub, step - 1].astype(F32)).astype(BF)
            ring_copy(quarter, step).start()
        return carry

    lax.fori_loop(1, 7, ring_step, 0)
    for quarter in ORDER_OF_QUARTERS:
        way, sub = stream(quarter)
        own = term(quarter, 7)
        ring_copy(quarter, 6).wait_recv()
        result = own + ring_recv[way, sub, 6].astype(F32)
        out[:, pl.ds(quarter * QUARTER, QUARTER)] = result.T.astype(BF)

    spread_done(prod_send, prod_ss)
    spread_done(filt_send, filt_ss)
    spread_done(conv_send, conv_ss)
    arrive(weights.at[pl.ds(0, 6)], weight_ss)
    for quarter in ORDER_OF_QUARTERS:
        way, sub = stream(quarter)
        gate_copy(0, quarter, 0, 2, across).wait_send()
        gate_copy(1, quarter, 0, 1, sibling).wait_send()
        gate_copy(2, quarter, 2, 3, sibling).wait_send()

        def sent(step, carry):
            ring_copy(quarter, step).wait_send()
            return carry

        lax.fori_loop(0, 7, sent, 0)


def body(query_input, key_input, value_input, filter_spectrum, out_weight):
    moves, long_table, twist, short_table = make_tables()
    filt = filter_spectrum.transpose(2, 1, 0, 3)
    anywhere = pl.BlockSpec(memory_space=pl.ANY)
    dma = pltpu.SemaphoreType.DMA
    return pl.pallas_call(
        kernel,
        out_shape=jax.ShapeDtypeStruct((256, 1024), BF),
        in_specs=[anywhere] * 9,
        out_specs=pl.BlockSpec(memory_space=pltpu.VMEM),
        scratch_shapes=[
            pltpu.VMEM((1024, 256), BF),
            pltpu.VMEM((1024, 256), BF),
            pltpu.VMEM((1024, 256), BF),
            pltpu.VMEM((2, SHORT, 128, 256), BF),
            pltpu.VMEM((3, 512, 512), BF),
            pltpu.VMEM((2, ORDER, ORDER), BF),
            pltpu.VMEM((2, ORDER, LANES), F32),
            pltpu.VMEM((2, 2 * LANES, 2 * LANES), BF),
            pltpu.VMEM((SHORT, 64, 256), BF),
            pltpu.VMEM((SEQ, 64, LANES), BF),
            pltpu.VMEM((SEQ, 64, LANES), BF),
            pltpu.VMEM((SEQ, 2, 128, LANES), BF),
            pltpu.VMEM((SEQ, 2, 128, LANES), BF),
            pltpu.VMEM((ORDER, 2 * LANES), F32),
            pltpu.VMEM((512, LANES), F32),
            pltpu.VMEM((SEQ, 64, LANES), BF),
            pltpu.VMEM((SEQ, 64, LANES), BF),
            pltpu.VMEM((1024, 1024), BF),
            pltpu.VMEM((8, 1024, 256), BF),
            pltpu.VMEM((2, 2, 7, QUARTER, 256), BF),
            pltpu.VMEM((2, 2, 7, QUARTER, 256), BF),
            dma((8,)),
            dma((SEQ,)),
            dma((SEQ,)),
            dma((SEQ,)),
            dma((SEQ,)),
            dma((SEQ,)),
            dma((SEQ,)),
            dma,
            dma((8,)),
            dma((3, 4)),
            dma((3, 4)),
            dma((2, 2, 7)),
            dma((2, 2, 7)),
        ],
        compiler_params=pltpu.CompilerParams(
            collective_id=0, has_side_effects=True, vmem_limit_bytes=58 * 2**20
        ),
        name="hyena",
    )(
        query_input,
        key_input,
        value_input,
        filt,
        out_weight,
        jnp.asarray(moves),
        jnp.asarray(long_table),
        jnp.asarray(twist),
        jnp.asarray(short_table),
    )


def solution(mesh):
    in_specs = (
        P("seq", "chan"),
        P("seq", "chan"),
        P("seq", "chan"),
        P("seq", None, None, "chan"),
        P("chan", None),
    )
    return jax.shard_map(
        body, mesh=mesh, in_specs=in_specs, out_specs=P("chan", "seq"), check_vma=False
    )
```

profile of v0, /device:TPU:8, one launch (start us, length us, event | category | flops | bytes accessed | tf_op | source)
XLA Modules:
  0.0 129.4 jit_solution(3513951538843205521)
XLA Ops:
  0.0 4.1 %copy.12 = bf16[128,16,2,256]{3,0,1,2:T(8,128)(2,1)} copy(bf16[128,16,2,256]{3,2,1,0:T(2,128)(2,1)} %param.12) | data formatting | bytes 4194304 | tf_op args[3]
  4.1 123.4 %hyena.1 = bf16[256,1024]{1,0:T(8,128)(2,1)} custom-call(bf16[1024,256]{1,0:T(8,128)(2,1)} %query.1, bf16[1024,256]{1,0:T(8,128)(2,1)} %key.1, bf16[1024,256]{1,0:T(8,128)(2,1)} %value.1, bf16[2,16,128,256]{3,2,1,0:T(8,128)(2,1)} %bitcast.3, bf16[256,8192]{1,0:T(8,128)(2,1)} %weight.1, bf16[3,512,512]{2,1,0:T(8,128)(2,1)} %constant.8.clone.moves, ...), custom_call_target="tpu_custom_call" | custom-call | tf_op jit(solution)/shard_map/hyena/pallas_call | solution.py:467
  127.5 1.9 %copy.14 = bf16[256,1024]{1,0:T(8,128)(2,1)} copy(bf16[256,1024]{1,0:T(8,128)(2,1)} %hyena.1) | data formatting | bytes 1048576
where the time goes:
time: 130 us; the launch traced here: 129 us
  Pallas kernels  123 us (95%)
  local copies, waits for them, and re-layouts  5.98 us (5%)
    pallas_call x1, Pallas kernels, body(): pl.pallas_call(kernel, out_shape=jax.ShapeDtypeStruct((256, 1024), BF), i...  123 us
    unnamed x2, local copies, waits for them, and re-layouts  5.98 us

commit v1 on v0

v1 whole, which is shorter than its diff:
```python
import functools
import math

import jax
import jax.numpy as jnp
import ml_dtypes
import numpy as np
from jax import lax
from jax.experimental import pallas as pl
from jax.experimental.pallas import tpu as pltpu
from jax.sharding import PartitionSpec as P

BF = jnp.bfloat16
F32 = jnp.float32
ORDER = 1024
SHORT = 16
TOTAL = ORDER * SHORT
SEQ = 8
SUB = 32
LANES = SHORT * SUB
MESH = pl.DeviceIdType.MESH
WAVES = 4
WAVE_ROWS = ORDER // SEQ // WAVES
STREAMS = 4
PIECE = 512 // STREAMS
PIECES = tuple(way * STREAMS + sub for sub in range(STREAMS) for way in range(2))


def make_tables():
    step = np.arange(ORDER)
    angle = 2.0 * math.pi / ORDER * (np.outer(step, step) % ORDER)
    order = step.reshape(SEQ, WAVES, WAVE_ROWS).transpose(1, 0, 2).ravel()
    long = np.stack([np.cos(angle), -np.sin(angle)])
    long_rows = long[:, order, : ORDER // 2]
    long_cols = long[:, : ORDER // 2, order]
    short = np.arange(SHORT)
    angle = 2.0 * math.pi / SHORT * (np.outer(short, short) % SHORT)
    eye = np.eye(SUB)
    short_cos = np.kron(np.cos(angle), eye)
    short_sin = np.kron(np.sin(angle), eye)
    forth = np.block([[short_cos, -short_sin], [short_sin, short_cos]])
    back = np.block([[short_cos, short_sin], [-short_sin, short_cos]])
    angle = 2.0 * math.pi / TOTAL * np.outer(step, short)[order]
    twist_cos = np.repeat(np.cos(angle), SUB, axis=1)
    twist_sin = np.repeat(np.sin(angle), SUB, axis=1)
    rows = np.zeros((512, 512))
    first, second = np.meshgrid(np.arange(32), np.arange(16), indexing="ij")
    rows[(second * 32 + first).ravel(), (first * 16 + second).ravel()] = 1.0
    filt_rows = np.zeros((512, 512))
    first, second, part = np.meshgrid(
        np.arange(16), np.arange(16), np.arange(2), indexing="ij"
    )
    filt_rows[
        (part * 256 + second * 16 + first).ravel(), (first * 32 + second * 2 + part).ravel()
    ] = 1.0
    lanes = np.zeros((512, 512))
    outer, inner, chan = np.meshgrid(np.arange(4), np.arange(4), np.arange(32), indexing="ij")
    lanes[
        (outer * 128 + inner * 32 + chan).ravel(), (inner * 128 + outer * 32 + chan).ravel()
    ] = 1.0

    def half(array):
        return array.astype(np.float32).astype(ml_dtypes.bfloat16)

    return (
        half(np.stack([rows, rows.T, lanes, filt_rows])),
        half(long_rows),
        half(long_cols),
        np.stack([twist_cos, twist_sin]).astype(np.float32),
        half(np.stack([forth, back])),
    )


def dot(left, right):
    return jnp.dot(left, right, preferred_element_type=F32)


def arrive(ref, sem):
    pltpu.make_async_copy(ref, ref, sem).wait()


def kernel(
    query,
    key,
    value,
    filt,
    weight,
    moves,
    rows_table,
    cols_table,
    twist,
    short_table,
    out,
    query_v,
    key_v,
    value_v,
    filt_v,
    moves_v,
    rows_v,
    cols_v,
    twist_v,
    short_v,
    sorted_v,
    filt_sorted,
    prod_send,
    prod_recv,
    filt_send,
    filt_recv,
    field,
    total,
    conv_send,
    conv_recv,
    gated,
    weights,
    ring_send,
    ring_recv,
    local_sem,
    prod_ss,
    prod_rs,
    filt_ss,
    filt_rs,
    conv_ss,
    conv_rs,
    weight_ss,
    weight_rs,
    gate_ss,
    gate_rs,
    ring_ss,
    ring_rs,
):
    chan = lax.axis_index("chan")
    me = lax.axis_index("seq")
    y_lo, z, core = chan // 16, (chan // 2) % 8, chan % 2
    y_hi, x = me // 4, me % 4

    def chan_of(low, depth, which):
        return (low * 8 + depth) * 2 + which

    sibling = {"chan": chan_of(y_lo, z, 1 - core), "seq": me}
    across = {"chan": chan_of(1 - y_lo, z, core), "seq": me}
    far = (1 - y_hi) * 4 + x
    z_up = (z + 1) % 8
    z_down = (z + 7) % 8
    up = {"chan": chan_of(y_lo, z_up, core), "seq": me}
    down = {"chan": chan_of(y_lo, z_down, core), "seq": me}

    local = [
        (key, key_v),
        (value, value_v),
        (moves, moves_v),
        (filt, filt_v),
        (rows_table, rows_v),
        (twist, twist_v),
        (short_table, short_v),
        (cols_table, cols_v),
        (query, query_v),
    ]

    def local_start(*places):
        for at in places:
            pltpu.make_async_copy(local[at][0], local[at][1], local_sem.at[at]).start()

    def local_done(*places):
        for at in places:
            pltpu.make_async_copy(local[at][0], local[at][1], local_sem.at[at]).wait()

    local_start(0, 1, 2, 3)

    barrier = pltpu.get_barrier_semaphore()

    def greet(step, carry):
        peer = (me + step) % SEQ
        pl.semaphore_signal(barrier, 1, device_id={"chan": chan, "seq": peer}, device_id_type=MESH)
        return carry

    lax.fori_loop(1, SEQ, greet, 0)
    for peer in (
        sibling,
        up,
        down,
        across,
        {"chan": chan_of(1 - y_lo, z, 1 - core), "seq": me},
        {"chan": chan_of(1 - y_lo, z, core), "seq": far},
        {"chan": chan_of(1 - y_lo, z, 1 - core), "seq": far},
    ):
        pl.semaphore_signal(barrier, 1, device_id=peer, device_id_type=MESH)

    pl.semaphore_wait(barrier, SEQ - 1 + 7)

    def weight_block(low, depth, which):
        at = pl.multiple_of(chan_of(low, depth, which) * 256, 256)
        return weight.at[:, pl.ds(at, 256)]

    def send_weight_near(depth):
        pltpu.make_async_copy(
            weight_block(y_lo, depth, core), weights.at[depth, pl.ds(0, 256), :], weight_rs.at[depth]
        ).start()
        pltpu.make_async_remote_copy(
            weight_block(y_lo, depth, 1 - core),
            weights.at[depth, pl.ds(256, 256), :],
            weight_ss,
            weight_rs.at[depth],
            device_id=sibling,
            device_id_type=MESH,
        ).start()

    def send_weight_across(depth, seq_to):
        for slot, which in ((2, core), (3, 1 - core)):
            pltpu.make_async_remote_copy(
                weight_block(1 - y_lo, depth, which),
                weights.at[depth, pl.ds(slot * 256, 256), :],
                weight_ss,
                weight_rs.at[depth],
                device_id={"chan": chan_of(1 - y_lo, z, which), "seq": seq_to},
                device_id_type=MESH,
            ).start()

    send_weight_across(z_up, me)
    send_weight_across(z_down, far)

    local_done(0, 1, 2)
    for half in range(2):
        rows = pl.ds(half * 512, 512)
        product = (key_v[rows, :].astype(F32) * value_v[rows, :].astype(F32)).astype(BF)
        moved = dot(moves_v[0], product).astype(BF)
        sorted_v[:, pl.ds(half * 32, 32), :] = moved.reshape(SHORT, 32, 256)
    for tile in range(2):
        block = jnp.concatenate(
            [
                jnp.concatenate(
                    [sorted_v[4 * group + b, :, pl.ds(tile * 128, 128)] for b in range(4)], axis=1
                )
                for group in range(4)
            ],
            axis=0,
        )
        moved = dot(block, moves_v[2]).astype(BF)
        for owner in range(4):
            for group in range(4):
                prod_send[4 * tile + owner, :, pl.ds(group * 128, 128)] = moved[
                    group * 64 : (group + 1) * 64, owner * 128 : (owner + 1) * 128
                ]

    def spread(send, recv, ss, rs):
        def one(step, carry):
            peer = (me + step) % SEQ
            pltpu.make_async_remote_copy(
                send.at[peer],
                recv.at[me],
                ss.at[peer],
                rs.at[me],
                device_id={"chan": chan, "seq": peer},
                device_id_type=MESH,
            ).start()
            return carry

        lax.fori_loop(1, SEQ, one, 0)
        pltpu.make_async_copy(send.at[me], recv.at[me], rs.at[me]).start()

    def spread_done(send, ss):
        def one(step, carry):
            peer = (me + step) % SEQ
            arrive(send.at[peer], ss.at[peer])
            return carry

        lax.fori_loop(1, SEQ, one, 0)

    spread(prod_send, prod_recv, prod_ss, prod_rs)

    local_start(4, 5, 6)
    local_done(3)

    def filt_copy(wave, peer):
        return pltpu.make_async_remote_copy(
            filt_send.at[wave, peer],
            filt_recv.at[wave, me],
            filt_ss.at[wave],
            filt_rs.at[wave],
            device_id={"chan": chan, "seq": peer},
            device_id_type=MESH,
        )

    def send_filter(wave, carry):
        for at in range(2):
            block = filt_v[pl.ds((2 * wave + at) * 16, 16)].reshape(512, 256)
            moved = dot(moves_v[3], block).astype(BF)
            filt_sorted[:, :, pl.ds(at * 16, 16), :] = moved.reshape(2, SHORT, 16, 256)
        for tile in range(2):
            block = jnp.concatenate(
                [
                    jnp.concatenate(
                        [
                            filt_sorted[at, 4 * group + b, :, pl.ds(tile * 128, 128)]
                            for b in range(4)
                        ],
                        axis=1,
                    )
                    for at in range(2)
                    for group in range(4)
                ],
                axis=0,
            )
            moved = dot(block, moves_v[2]).astype(BF)
            for owner in range(4):
                for at in range(2):
                    for group in range(4):
                        first = (at * 4 + group) * WAVE_ROWS
                        filt_send[
                            wave, 4 * tile + owner, at, :, pl.ds(group * 128, 128)
                        ] = moved[first : first + WAVE_ROWS, owner * 128 : (owner + 1) * 128]

        def one(step, carry):
            filt_copy(wave, (me + step) % SEQ).start()
            return carry

        lax.fori_loop(1, SEQ, one, 0)
        pltpu.make_async_copy(
            filt_send.at[wave, me], filt_recv.at[wave, me], filt_rs.at[wave]
        ).start()
        return carry

    lax.fori_loop(0, WAVES, send_filter, 0)
    local_start(7, 8)

    def near_weights(depth, carry):
        send_weight_near(depth)
        return carry

    lax.fori_loop(0, 8, near_weights, 0)

    local_done(4, 5, 6)

    def wait_product(peer, carry):
        arrive(prod_recv.at[peer], prod_rs.at[peer])
        return carry

    lax.fori_loop(0, SEQ, wait_product, 0)

    def forward(step, carry):
        rows = pl.ds(pl.multiple_of(step * 256, 256), 256)
        values = prod_recv[...].reshape(512, LANES)
        real = dot(rows_v[0, rows, :], values)
        imag = dot(rows_v[1, rows, :], values)
        tw_cos = twist_v[0, rows, :]
        tw_sin = twist_v[1, rows, :]
        both = jnp.concatenate(
            [
                (real * tw_cos + imag * tw_sin).astype(BF),
                (imag * tw_cos - real * tw_sin).astype(BF),
            ],
            axis=1,
        )
        field[rows, :] = dot(both, short_v[0])
        return carry

    lax.fori_loop(0, 4, forward, 0)

    total[...] = jnp.zeros_like(total)
    local_done(7)

    def backward(wave, carry):
        arrive(filt_recv.at[wave], filt_rs.at[wave])
        rows = pl.ds(pl.multiple_of(wave * 256, 256), 256)
        real = field[rows, pl.ds(0, LANES)]
        imag = field[rows, pl.ds(LANES, LANES)]
        filt_real = filt_recv[wave, :, 0].reshape(256, LANES).astype(F32)
        filt_imag = filt_recv[wave, :, 1].reshape(256, LANES).astype(F32)
        both = jnp.concatenate(
            [
                (real * filt_real - imag * filt_imag).astype(BF),
                (real * filt_imag + imag * filt_real).astype(BF),
            ],
            axis=1,
        )
        mixed = dot(both, short_v[1])
        real = mixed[:, :LANES]
        imag = mixed[:, LANES:]
        tw_cos = twist_v[0, rows, :]
        tw_sin = twist_v[1, rows, :]
        turned = jnp.concatenate(
            [
                (real * tw_cos - imag * tw_sin).astype(BF),
                (imag * tw_cos + real * tw_sin).astype(BF),
            ],
            axis=0,
        )
        table = jnp.concatenate([cols_v[0, :, rows], cols_v[1, :, rows]], axis=1)
        total[...] += dot(table, turned)
        return carry

    lax.fori_loop(0, WAVES, backward, 0)
    conv_send[...] = (total[...] * (1.0 / TOTAL)).astype(BF).reshape(SEQ, 64, LANES)
    spread(conv_send, conv_recv, conv_ss, conv_rs)

    local_done(8)

    def wait_conv(peer, carry):
        arrive(conv_recv.at[peer], conv_rs.at[peer])
        return carry

    lax.fori_loop(0, SEQ, wait_conv, 0)
    for tile in range(2):
        block = jnp.concatenate(
            [
                jnp.concatenate(
                    [conv_recv[4 * tile + owner, :, pl.ds(group * 128, 128)] for owner in range(4)],
                    axis=1,
                )
                for group in range(4)
            ],
            axis=0,
        )
        moved = dot(block, moves_v[2]).astype(BF)
        for group in range(4):
            for b in range(4):
                sorted_v[4 * group + b, :, pl.ds(tile * 128, 128)] = moved[
                    group * 64 : (group + 1) * 64, b * 128 : (b + 1) * 128
                ]
    for half in range(2):
        rows = pl.ds(half * 512, 512)
        block = sorted_v[:, pl.ds(half * 32, 32), :].reshape(512, 256)
        conv = dot(moves_v[1], block)
        gated[rows, pl.ds(0, 256)] = (query_v[rows, :].astype(F32) * conv).astype(BF)

    def part(piece, slot):
        return gated.at[pl.ds(piece * PIECE, PIECE), pl.ds(slot * 256, 256)]

    def gate_copy(kind, piece, source, target, device):
        return pltpu.make_async_remote_copy(
            part(piece, source),
            part(piece, target),
            gate_ss.at[kind, piece],
            gate_rs.at[kind, piece],
            device_id=device,
            device_id_type=MESH,
        )

    for piece in PIECES:
        gate_copy(0, piece, 0, 2, across).start()
        gate_copy(1, piece, 0, 1, sibling).start()

    send_weight_across((z + 2) % 8, far)
    send_weight_across((z + 6) % 8, far)
    send_weight_across((z + 3) % 8, me)
    send_weight_across((z + 5) % 8, far)
    send_weight_across((z + 4) % 8, me)
    send_weight_across(z, far)

    def wait_weight(depth):
        arrive(weights.at[depth], weight_rs.at[depth])

    def block_at(piece, step):
        if piece // STREAMS == 0:
            return (z + 15 - step) % 8
        return (z + 1 + step) % 8

    def term(piece, step):
        rows = pl.ds(piece * PIECE, PIECE)
        return dot(gated[rows, :], weights[block_at(piece, step)])

    def ring_copy(piece, step):
        return pltpu.make_async_remote_copy(
            ring_send.at[piece, step],
            ring_recv.at[piece, step],
            ring_ss.at[piece, step],
            ring_rs.at[piece, step],
            device_id=up if piece // STREAMS == 0 else down,
            device_id_type=MESH,
        )

    wait_weight(z_up)
    wait_weight(z_down)
    for piece in PIECES:
        arrive(part(piece, 2), gate_rs.at[0, piece])
        gate_copy(2, piece, 2, 3, sibling).start()
        arrive(part(piece, 1), gate_rs.at[1, piece])
        arrive(part(piece, 3), gate_rs.at[2, piece])
        ring_send[piece, 0] = term(piece, 0).astype(BF)
        ring_copy(piece, 0).start()

    def ring_step(step, carry):
        @pl.when(step < 4)
        def _():
            wait_weight((z + 1 + step) % 8)

        @pl.when(step < 3)
        def _():
            wait_weight((z + 7 - step) % 8)

        for piece in PIECES:
            own = term(piece, step)
            ring_copy(piece, step - 1).wait_recv()
            ring_send[piece, step] = (own + ring_recv[piece, step - 1].astype(F32)).astype(BF)
            ring_copy(piece, step).start()
        return carry

    lax.fori_loop(1, 7, ring_step, 0)
    wait_weight(z)
    for piece in PIECES:
        own = term(piece, 7)
        ring_copy(piece, 6).wait_recv()
        result = own + ring_recv[piece, 6].astype(F32)
        out[pl.ds(piece * PIECE, PIECE), :] = result.astype(BF)

    spread_done(prod_send, prod_ss)
    spread_done(conv_send, conv_ss)

    def filter_sent(wave, carry):
        arrive(filt_send.at[wave, pl.ds(0, SEQ - 1)], filt_ss.at[wave])
        return carry

    lax.fori_loop(0, WAVES, filter_sent, 0)
    arrive(weights.at[pl.ds(0, 6)], weight_ss)
    for piece in PIECES:
        gate_copy(0, piece, 0, 2, across).wait_send()
        gate_copy(1, piece, 0, 1, sibling).wait_send()
        gate_copy(2, piece, 2, 3, sibling).wait_send()

        def sent(step, carry):
            ring_copy(piece, step).wait_send()
            return carry

        lax.fori_loop(0, 7, sent, 0)


def body(query_input, key_input, value_input, filter_spectrum, out_weight):
    moves, rows_table, cols_table, twist, short_table = make_tables()
    anywhere = pl.BlockSpec(memory_space=pl.ANY)
    dma = pltpu.SemaphoreType.DMA
    mixed = pl.pallas_call(
        kernel,
        out_shape=pltpu.VMEM((1024, 256), BF),
        in_specs=[anywhere] * 10,
        out_specs=pl.BlockSpec(memory_space=pltpu.VMEM),
        scratch_shapes=[
            pltpu.VMEM((1024, 256), BF),
            pltpu.VMEM((1024, 256), BF),
            pltpu.VMEM((1024, 256), BF),
            pltpu.VMEM((128, SHORT, 2, 256), BF),
            pltpu.VMEM((4, 512, 512), BF),
            pltpu.VMEM((2, ORDER, ORDER // 2), BF),
            pltpu.VMEM((2, ORDER // 2, ORDER), BF),
            pltpu.VMEM((2, ORDER, LANES), F32),
            pltpu.VMEM((2, 2 * LANES, 2 * LANES), BF),
            pltpu.VMEM((SHORT, 64, 256), BF),
            pltpu.VMEM((2, SHORT, WAVE_ROWS, 256), BF),
            pltpu.VMEM((SEQ, 64, LANES), BF),
            pltpu.VMEM((SEQ, 64, LANES), BF),
            pltpu.VMEM((WAVES, SEQ, 2, WAVE_ROWS, LANES), BF),
            pltpu.VMEM((WAVES, SEQ, 2, WAVE_ROWS, LANES), BF),
            pltpu.VMEM((ORDER, 2 * LANES), F32),
            pltpu.VMEM((512, LANES), F32),
            pltpu.VMEM((SEQ, 64, LANES), BF),
            pltpu.VMEM((SEQ, 64, LANES), BF),
            pltpu.VMEM((1024, 1024), BF),
            pltpu.VMEM((8, 1024, 256), BF),
            pltpu.VMEM((2 * STREAMS, 7, PIECE, 256), BF),
            pltpu.VMEM((2 * STREAMS, 7, PIECE, 256), BF),
            dma((9,)),
            dma((SEQ,)),
            dma((SEQ,)),
            dma((WAVES,)),
            dma((WAVES,)),
            dma((SEQ,)),
            dma((SEQ,)),
            dma,
            dma((8,)),
            dma((3, 2 * STREAMS)),
            dma((3, 2 * STREAMS)),
            dma((2 * STREAMS, 7)),
            dma((2 * STREAMS, 7)),
        ],
        compiler_params=pltpu.CompilerParams(
            collective_id=0, has_side_effects=True, vmem_limit_bytes=58 * 2**20
        ),
        name="hyena",
    )(
        query_input,
        key_input,
        value_input,
        filter_spectrum,
        out_weight,
        jnp.asarray(moves),
        jnp.asarray(rows_table),
        jnp.asarray(cols_table),
        jnp.asarray(twist),
        jnp.asarray(short_table),
    )
    return mixed.T


def solution(mesh):
    in_specs = (
        P("seq", "chan"),
        P("seq", "chan"),
        P("seq", "chan"),
        P("seq", None, None, "chan"),
        P("chan", None),
    )
    return jax.shard_map(
        body, mesh=mesh, in_specs=in_specs, out_specs=P("chan", "seq"), check_vma=False
    )
```

time: 130 us -> 114 us (0.88)
  Pallas kernels: 123 us -> 111 us
  local copies, waits for them, and re-layouts: 5.98 us -> 1 us
    pallas_call x1, Pallas kernels: 123 us -> 111 us  [body(): pl.pallas_call(kernel, out_shape=pltpu.VMEM((1024, 256), BF), in_specs=[a...]
    unnamed x2 -> x0, local copies, waits for them, and re-layouts: 5.98 us -> none
where the time goes in v1:
time: 114 us; the launch traced here: 112 us
  Pallas kernels  111 us (97%)
    pallas_call x1, Pallas kernels, body(): pl.pallas_call(kernel, out_shape=pltpu.VMEM((1024, 256), BF), in_specs=[a...  111 us

profile of v1, /device:TPU:8, one launch (start us, length us, event | category | flops | bytes accessed | tf_op | source)
XLA Modules:
  0.0 112.5 jit_solution(14487373399459800171)
XLA Ops:
  0.0 111.5 %hyena.1 = bf16[1024,256]{1,0:T(8,128)(2,1)S(1)} custom-call(bf16[1024,256]{1,0:T(8,128)(2,1)} %query.1, bf16[1024,256]{1,0:T(8,128)(2,1)} %key.1, bf16[1024,256]{1,0:T(8,128)(2,1)} %value.1, bf16[128,16,2,256]{3,2,1,0:T(2,128)(2,1)} %filt.1, bf16[256,8192]{1,0:T(8,128)(2,1)} %weight.1, bf16[4,512,512]{2,1,0:T(8,128)(2,1)} %constant.10.clone.moves, ...), custom_call_target="tpu_custom_call" | custom-call | tf_op jit(solution)/shard_map/hyena/pallas_call | solution.py:530
  111.5 1.0 copy.11

commit v2 on v1

v2 whole, which is shorter than its diff:
```python
import functools
import math

import jax
import jax.numpy as jnp
import ml_dtypes
import numpy as np
from jax import lax
from jax.experimental import pallas as pl
from jax.experimental.pallas import tpu as pltpu
from jax.sharding import PartitionSpec as P

BF = jnp.bfloat16
F32 = jnp.float32
ORDER = 1024
SHORT = 16
TOTAL = ORDER * SHORT
SEQ = 8
SHARES = 2
SUB = 16
LANES = SHORT * SUB
MESH = pl.DeviceIdType.MESH
WAVES = 4
WAVE_ROWS = ORDER // SEQ // WAVES
STREAMS = 4
PIECE = 512 // STREAMS


def make_tables():
    step = np.arange(ORDER)
    angle = 2.0 * math.pi / ORDER * (np.outer(step, step) % ORDER)
    order = step.reshape(SEQ, WAVES, WAVE_ROWS).transpose(1, 0, 2).ravel()
    long = np.stack([np.cos(angle), -np.sin(angle)])
    long_rows = long[:, order, : ORDER // 2]
    long_cols = long[:, : ORDER // 2, order]
    short = np.arange(SHORT)
    angle = 2.0 * math.pi / SHORT * (np.outer(short, short) % SHORT)
    eye = np.eye(SUB)
    short_cos = np.kron(np.cos(angle), eye)
    short_sin = np.kron(np.sin(angle), eye)
    forth = np.block([[short_cos, -short_sin], [short_sin, short_cos]])
    back = np.block([[short_cos, short_sin], [-short_sin, short_cos]])
    angle = 2.0 * math.pi / TOTAL * np.outer(step, short)[order]
    twist_cos = np.repeat(np.cos(angle), SUB, axis=1)
    twist_sin = np.repeat(np.sin(angle), SUB, axis=1)
    rows = np.zeros((512, 512))
    first, second = np.meshgrid(np.arange(32), np.arange(16), indexing="ij")
    rows[(second * 32 + first).ravel(), (first * 16 + second).ravel()] = 1.0
    filt_rows = np.zeros((512, 512))
    first, second, part = np.meshgrid(
        np.arange(16), np.arange(16), np.arange(2), indexing="ij"
    )
    filt_rows[
        (part * 256 + second * 16 + first).ravel(), (first * 32 + second * 2 + part).ravel()
    ] = 1.0
    lanes = np.zeros((1024, 1024))
    outer, inner, chan = np.meshgrid(np.arange(8), np.arange(8), np.arange(16), indexing="ij")
    lanes[
        (outer * 128 + inner * 16 + chan).ravel(), (inner * 128 + outer * 16 + chan).ravel()
    ] = 1.0

    def half(array):
        return array.astype(np.float32).astype(ml_dtypes.bfloat16)

    return (
        half(np.stack([rows, rows.T, filt_rows])),
        half(lanes),
        half(long_rows),
        half(long_cols),
        np.stack([twist_cos, twist_sin]).astype(np.float32),
        half(np.stack([forth, back])),
    )


def dot(left, right):
    return jnp.dot(left, right, preferred_element_type=F32)


def arrive(ref, sem):
    pltpu.make_async_copy(ref, ref, sem).wait()


def kernel(
    query,
    key,
    value,
    filt,
    weight,
    moves,
    lanes_table,
    rows_table,
    cols_table,
    twist,
    short_table,
    out,
    query_v,
    key_v,
    value_v,
    filt_v,
    moves_v,
    lanes_v,
    rows_v,
    cols_v,
    twist_v,
    short_v,
    sorted_v,
    filt_sorted,
    prod_send,
    prod_recv,
    filt_send,
    filt_recv,
    field,
    total,
    conv_send,
    conv_recv,
    gated,
    weights,
    ring_send,
    ring_recv,
    local_sem,
    prod_ss,
    prod_rs,
    filt_ss,
    filt_rs,
    conv_ss,
    conv_rs,
    weight_ss,
    weight_rs,
    share_rs,
    gate_ss,
    gate_rs,
    ring_ss,
    ring_rs,
):
    chan = lax.axis_index("chan")
    me = lax.axis_index("seq")
    y_lo, z, core = chan // 16, (chan // 2) % 8, chan % 2
    y_hi, x = me // 4, me % 4

    def chan_of(low, depth, which):
        return (low * 8 + depth) * 2 + which

    sibling = {"chan": chan_of(y_lo, z, 1 - core), "seq": me}
    across = {"chan": chan_of(1 - y_lo, z, core), "seq": me}
    far = (1 - y_hi) * 4 + x
    z_up = (z + 1) % 8
    z_down = (z + 7) % 8

    local = [
        (key, key_v),
        (value, value_v),
        (moves, moves_v),
        (lanes_table, lanes_v),
        (filt, filt_v),
        (rows_table, rows_v),
        (twist, twist_v),
        (short_table, short_v),
        (cols_table, cols_v),
        (query, query_v),
    ]

    def local_start(*places):
        for at in places:
            pltpu.make_async_copy(local[at][0], local[at][1], local_sem.at[at]).start()

    def local_done(*places):
        for at in places:
            pltpu.make_async_copy(local[at][0], local[at][1], local_sem.at[at]).wait()

    local_start(0, 1, 2, 3, 4)

    barrier = pltpu.get_barrier_semaphore()

    def greet(step, carry):
        peer = (me + step) % SEQ
        pl.semaphore_signal(barrier, 1, device_id={"chan": chan, "seq": peer}, device_id_type=MESH)
        return carry

    lax.fori_loop(1, SEQ, greet, 0)
    for peer in (
        sibling,
        {"chan": chan_of(y_lo, z_up, core), "seq": me},
        {"chan": chan_of(y_lo, z_down, core), "seq": me},
        across,
        {"chan": chan_of(1 - y_lo, z, 1 - core), "seq": me},
        {"chan": chan_of(1 - y_lo, z, core), "seq": far},
        {"chan": chan_of(1 - y_lo, z, 1 - core), "seq": far},
    ):
        pl.semaphore_signal(barrier, 1, device_id=peer, device_id_type=MESH)

    pl.semaphore_wait(barrier, SEQ - 1 + 7)

    def weight_block(low, depth, which):
        at = pl.multiple_of(chan_of(low, depth, which) * 256, 256)
        return weight.at[:, pl.ds(at, 256)]

    def send_weight_near(depth):
        pltpu.make_async_copy(
            weight_block(y_lo, depth, core), weights.at[depth, pl.ds(0, 256), :], weight_rs.at[depth]
        ).start()
        pltpu.make_async_remote_copy(
            weight_block(y_lo, depth, 1 - core),
            weights.at[depth, pl.ds(256, 256), :],
            weight_ss,
            weight_rs.at[depth],
            device_id=sibling,
            device_id_type=MESH,
        ).start()

    core_across = (core + x // 2) % 2
    row_across = pl.multiple_of((x % 2) * 128, 128)
    row_shared = pl.multiple_of(512 + x * 128, 128)

    def send_weight_across(step, seq_to):
        depth = (z + step) % 8
        at = pl.multiple_of(chan_of(1 - y_lo, depth, core_across) * 256, 256)
        pltpu.make_async_remote_copy(
            weight.at[pl.ds(row_across, 128), pl.ds(at, 256)],
            weights.at[depth, pl.ds(row_shared, 128), :],
            weight_ss,
            share_rs,
            device_id={"chan": chan_of(1 - y_lo, z, core_across), "seq": seq_to},
            device_id_type=MESH,
        ).start()

    def share_weight(step):
        depth = (z + step) % 8
        shared = weights.at[depth, pl.ds(row_shared, 128), :]
        for peer in (1, 3, 2):
            pltpu.make_async_remote_copy(
                shared,
                shared,
                weight_ss,
                weight_rs.at[depth],
                device_id={"chan": chan, "seq": y_hi * 4 + (x + peer) % 4},
                device_id_type=MESH,
            ).start()

    for step, seq_to in ((1, me), (7, far), (2, far), (6, me), (3, me), (5, far), (4, me), (0, far)):
        send_weight_across(step, seq_to)

    local_done(0, 1, 2)
    for half in range(2):
        rows = pl.ds(half * 512, 512)
        product = (key_v[rows, :].astype(F32) * value_v[rows, :].astype(F32)).astype(BF)
        moved = dot(moves_v[0], product).astype(BF)
        sorted_v[:, pl.ds(half * 32, 32), :] = moved.reshape(SHORT, 32, 256)
    local_done(3)
    for share in range(SHARES):
        block = jnp.concatenate(
            [
                jnp.concatenate(
                    [sorted_v[8 * group + b, :, pl.ds(share * 128, 128)] for b in range(8)], axis=1
                )
                for group in range(2)
            ],
            axis=0,
        )
        moved = dot(block, lanes_v[...]).astype(BF)
        for owner in range(SEQ):
            for group in range(2):
                prod_send[share, owner, :, pl.ds(group * 128, 128)] = moved[
                    group * 64 : (group + 1) * 64, owner * 128 : (owner + 1) * 128
                ]


    def spread(send, recv, ss, rs):
        def one(step, carry):
            peer = (me + step) % SEQ
            pltpu.make_async_remote_copy(
                send.at[peer],
                recv.at[me],
                ss,
                rs,
                device_id={"chan": chan, "seq": peer},
                device_id_type=MESH,
            ).start()
            return carry

        lax.fori_loop(1, SEQ, one, 0)
        pltpu.make_async_copy(send.at[me], recv.at[me], rs).start()

    for share in range(SHARES):
        spread(prod_send.at[share], prod_recv.at[share], prod_ss.at[share], prod_rs.at[share])

    local_start(5, 6, 7)
    local_done(4)

    def send_filter(share, wave):
        block = jnp.concatenate(
            [
                jnp.concatenate(
                    [
                        filt_sorted[wave, at, 8 * group + b, :, pl.ds(share * 128, 128)]
                        for b in range(8)
                    ],
                    axis=1,
                )
                for at in range(2)
                for group in range(2)
            ],
            axis=0,
        )
        moved = dot(block, lanes_v[...]).astype(BF)
        for owner in range(SEQ):
            for at in range(2):
                for group in range(2):
                    first = (at * 2 + group) * WAVE_ROWS
                    filt_send[share, wave, owner, at, :, pl.ds(group * 128, 128)] = moved[
                        first : first + WAVE_ROWS, owner * 128 : (owner + 1) * 128
                    ]
        spread(
            filt_send.at[share, wave],
            filt_recv.at[share, wave],
            filt_ss.at[share, wave],
            filt_rs.at[share, wave],
        )

    def sort_filter(wave, carry):
        for at in range(2):
            block = filt_v[pl.ds((2 * wave + at) * 16, 16)].reshape(512, 256)
            moved = dot(moves_v[2], block).astype(BF)
            filt_sorted[wave, :, :, pl.ds(at * 16, 16), :] = moved.reshape(2, SHORT, 16, 256)
        send_filter(0, wave)
        return carry

    def rest_of_filter(wave, carry):
        send_filter(1, wave)
        return carry

    lax.fori_loop(0, WAVES, sort_filter, 0)
    lax.fori_loop(0, WAVES, rest_of_filter, 0)
    local_start(8, 9)

    def near_weights(depth, carry):
        send_weight_near(depth)
        return carry

    lax.fori_loop(0, 8, near_weights, 0)
    arrive(weights.at[0], share_rs)
    share_weight(1)
    share_weight(7)

    local_done(5, 6, 7)

    def forward(at, carry):
        share, step = at // 4, at % 4

        @pl.when(step == 0)
        def _():
            arrive(prod_recv.at[share], prod_rs.at[share])

        rows = pl.ds(pl.multiple_of(step * 256, 256), 256)
        values = prod_recv[share].reshape(512, LANES)
        real = dot(rows_v[0, rows, :], values)
        imag = dot(rows_v[1, rows, :], values)
        tw_cos = twist_v[0, rows, :]
        tw_sin = twist_v[1, rows, :]
        both = jnp.concatenate(
            [
                (real * tw_cos + imag * tw_sin).astype(BF),
                (imag * tw_cos - real * tw_sin).astype(BF),
            ],
            axis=1,
        )
        field[share, rows, :] = dot(both, short_v[0])
        return carry

    lax.fori_loop(0, SHARES * 4, forward, 0)
    local_done(8)

    def inverse(share):
        total[...] = jnp.zeros_like(total)

        def backward(wave, carry):
            arrive(filt_recv.at[share, wave], filt_rs.at[share, wave])
            rows = pl.ds(pl.multiple_of(wave * 256, 256), 256)
            real = field[share, rows, pl.ds(0, LANES)]
            imag = field[share, rows, pl.ds(LANES, LANES)]
            filt_real = filt_recv[share, wave, :, 0].reshape(256, LANES).astype(F32)
            filt_imag = filt_recv[share, wave, :, 1].reshape(256, LANES).astype(F32)
            both = jnp.concatenate(
                [
                    (real * filt_real - imag * filt_imag).astype(BF),
                    (real * filt_imag + imag * filt_real).astype(BF),
                ],
                axis=1,
            )
            mixed = dot(both, short_v[1])
            real = mixed[:, :LANES]
            imag = mixed[:, LANES:]
            tw_cos = twist_v[0, rows, :]
            tw_sin = twist_v[1, rows, :]
            turned = jnp.concatenate(
                [
                    (real * tw_cos - imag * tw_sin).astype(BF),
                    (imag * tw_cos + real * tw_sin).astype(BF),
                ],
                axis=0,
            )
            table = jnp.concatenate([cols_v[0, :, rows], cols_v[1, :, rows]], axis=1)
            total[...] += dot(table, turned)
            return carry

        lax.fori_loop(0, WAVES, backward, 0)
        conv_send[share] = (total[...] * (1.0 / TOTAL)).astype(BF).reshape(SEQ, 64, LANES)
        spread(conv_send.at[share], conv_recv.at[share], conv_ss.at[share], conv_rs.at[share])

    def rows_of(piece):
        return pl.ds(pl.multiple_of(piece * PIECE, PIECE), PIECE)

    def part(piece, slot, share):
        return gated.at[rows_of(piece), pl.ds(slot * 256 + share * 128, 128)]

    def gate_copy(kind, piece, share, source, target, device):
        return pltpu.make_async_remote_copy(
            part(piece, source, share),
            part(piece, target, share),
            gate_ss.at[kind, share],
            gate_rs.at[kind, share, piece],
            device_id=device,
            device_id_type=MESH,
        )

    def piece_of(at):
        return (at % 2) * STREAMS + at // 2

    def gate(share):
        arrive(conv_recv.at[share], conv_rs.at[share])
        lanes = pl.ds(share * 128, 128)
        block = jnp.concatenate(
            [
                jnp.concatenate(
                    [conv_recv[share, owner, :, pl.ds(group * 128, 128)] for owner in range(SEQ)],
                    axis=1,
                )
                for group in range(2)
            ],
            axis=0,
        )
        moved = dot(block, lanes_v[...]).astype(BF)
        for group in range(2):
            for b in range(8):
                sorted_v[8 * group + b, :, lanes] = moved[
                    group * 64 : (group + 1) * 64, b * 128 : (b + 1) * 128
                ]
        for half in range(2):
            rows = pl.ds(half * 512, 512)
            block = sorted_v[:, pl.ds(half * 32, 32), lanes].reshape(512, 128)
            conv = dot(moves_v[1], block)
            gated[rows, lanes] = (query_v[rows, lanes].astype(F32) * conv).astype(BF)

        def send_gated(at, carry):
            piece = piece_of(at)
            gate_copy(0, piece, share, 0, 2, across).start()
            gate_copy(1, piece, share, 0, 1, sibling).start()
            return carry

        lax.fori_loop(0, 2 * STREAMS, send_gated, 0)

    def pass_on(piece, share):
        arrive(part(piece, 2, share), gate_rs.at[0, share, piece])
        gate_copy(2, piece, share, 2, 3, sibling).start()

    def gate_done(piece, share):
        arrive(part(piece, 1, share), gate_rs.at[1, share, piece])
        arrive(part(piece, 3, share), gate_rs.at[2, share, piece])

    local_done(9)
    inverse(0)
    inverse(1)
    gate(0)
    share_weight(2)
    share_weight(6)

    def pass_first(at, carry):
        pass_on(piece_of(at), 0)
        return carry

    gate(1)
    lax.fori_loop(0, 2 * STREAMS, pass_first, 0)
    for step in (3, 5, 4, 0):
        share_weight(step)

    def wait_weight(step):
        depth = (z + step) % 8
        arrive(weights.at[depth, pl.ds(0, 896), :], weight_rs.at[depth])

    def term(piece, step):
        depth = (z + 7 - step) % 8 if piece // STREAMS == 0 else (z + 1 + step) % 8
        return dot(gated[rows_of(piece), :], weights[depth])

    def ring_copy(piece, step):
        depth = z_up if piece // STREAMS == 0 else z_down
        return pltpu.make_async_remote_copy(
            ring_send.at[piece, step],
            ring_recv.at[piece, step],
            ring_ss.at[piece],
            ring_rs.at[piece, step],
            device_id={"chan": chan_of(y_lo, depth, core), "seq": me},
            device_id_type=MESH,
        )

    wait_weight(1)
    wait_weight(7)
    for sub in range(STREAMS):
        for piece in (sub, sub + STREAMS):
            pass_on(piece, 1)
        for piece in (sub, sub + STREAMS):
            gate_done(piece, 0)
            gate_done(piece, 1)
            ring_send[piece, 0] = term(piece, 0).astype(BF)
            ring_copy(piece, 0).start()

    def ring_step(step, carry):
        @pl.when(step < 4)
        def _():
            wait_weight(1 + step)

        @pl.when(step < 3)
        def _():
            wait_weight(7 - step)

        for sub in range(STREAMS):
            for piece in (sub, sub + STREAMS):
                own = term(piece, step)
                ring_copy(piece, step - 1).wait_recv()
                ring_send[piece, step] = (own + ring_recv[piece, step - 1].astype(F32)).astype(BF)
                ring_copy(piece, step).start()
        return carry

    lax.fori_loop(1, 7, ring_step, 0)
    wait_weight(0)
    for sub in range(STREAMS):
        for piece in (sub, sub + STREAMS):
            own = term(piece, 7)
            ring_copy(piece, 6).wait_recv()
            out[rows_of(piece), :] = (own + ring_recv[piece, 6].astype(F32)).astype(BF)

    for share in range(SHARES):
        arrive(prod_send.at[share, pl.ds(0, SEQ - 1)], prod_ss.at[share])
        arrive(conv_send.at[share, pl.ds(0, SEQ - 1)], conv_ss.at[share])
        for wave in range(WAVES):
            arrive(filt_send.at[share, wave, pl.ds(0, SEQ - 1)], filt_ss.at[share, wave])
        for kind in range(3):
            arrive(gated.at[:, pl.ds(0, 128)], gate_ss.at[kind, share])
    arrive(weights.at[pl.ds(0, 6)], weight_ss)
    for piece in range(2 * STREAMS):
        arrive(ring_send.at[piece], ring_ss.at[piece])


def body(query_input, key_input, value_input, filter_spectrum, out_weight):
    moves, lanes_table, rows_table, cols_table, twist, short_table = make_tables()
    anywhere = pl.BlockSpec(memory_space=pl.ANY)
    dma = pltpu.SemaphoreType.DMA
    mixed = pl.pallas_call(
        kernel,
        out_shape=pltpu.VMEM((1024, 256), BF),
        in_specs=[anywhere] * 11,
        out_specs=pl.BlockSpec(memory_space=pltpu.VMEM),
        scratch_shapes=[
            pltpu.VMEM((1024, 256), BF),
            pltpu.VMEM((1024, 256), BF),
            pltpu.VMEM((1024, 256), BF),
            pltpu.VMEM((128, SHORT, 2, 256), BF),
            pltpu.VMEM((3, 512, 512), BF),
            pltpu.VMEM((1024, 1024), BF),
            pltpu.VMEM((2, ORDER, ORDER // 2), BF),
            pltpu.VMEM((2, ORDER // 2, ORDER), BF),
            pltpu.VMEM((2, ORDER, LANES), F32),
            pltpu.VMEM((2, 2 * LANES, 2 * LANES), BF),
            pltpu.VMEM((SHORT, 64, 256), BF),
            pltpu.VMEM((WAVES, 2, SHORT, WAVE_ROWS, 256), BF),
            pltpu.VMEM((SHARES, SEQ, 64, LANES), BF),
            pltpu.VMEM((SHARES, SEQ, 64, LANES), BF),
            pltpu.VMEM((SHARES, WAVES, SEQ, 2, WAVE_ROWS, LANES), BF),
            pltpu.VMEM((SHARES, WAVES, SEQ, 2, WAVE_ROWS, LANES), BF),
            pltpu.VMEM((SHARES, ORDER, 2 * LANES), F32),
            pltpu.VMEM((512, LANES), F32),
            pltpu.VMEM((SHARES, SEQ, 64, LANES), BF),
            pltpu.VMEM((SHARES, SEQ, 64, LANES), BF),
            pltpu.VMEM((1024, 1024), BF),
            pltpu.VMEM((8, 1024, 256), BF),
            pltpu.VMEM((2 * STREAMS, 7, PIECE, 256), BF),
            pltpu.VMEM((2 * STREAMS, 7, PIECE, 256), BF),
            dma((10,)),
            dma((SHARES,)),
            dma((SHARES,)),
            dma((SHARES, WAVES)),
            dma((SHARES, WAVES)),
            dma((SHARES,)),
            dma((SHARES,)),
            dma,
            dma((8,)),
            dma,
            dma((3, SHARES)),
            dma((3, SHARES, 2 * STREAMS)),
            dma((2 * STREAMS,)),
            dma((2 * STREAMS, 7)),
        ],
        compiler_params=pltpu.CompilerParams(
            collective_id=0, has_side_effects=True, vmem_limit_bytes=58 * 2**20
        ),
        name="hyena",
    )(
        query_input,
        key_input,
        value_input,
        filter_spectrum,
        out_weight,
        jnp.asarray(moves),
        jnp.asarray(lanes_table),
        jnp.asarray(rows_table),
        jnp.asarray(cols_table),
        jnp.asarray(twist),
        jnp.asarray(short_table),
    )
    return mixed.T


def solution(mesh):
    in_specs = (
        P("seq", "chan"),
        P("seq", "chan"),
        P("seq", "chan"),
        P("seq", None, None, "chan"),
        P("chan", None),
    )
    return jax.shard_map(
        body, mesh=mesh, in_specs=in_specs, out_specs=P("chan", "seq"), check_vma=False
    )
```

time: 114 us -> 110 us (0.965); the launches traced: 112 us -> 110 us
  Pallas kernels: 111 us -> 109 us
    pallas_call x1, Pallas kernels: 111 us -> 109 us  [body(): pl.pallas_call(kernel, out_shape=pltpu.VMEM((1024, 256), BF), in_specs=[a...]
where the time goes in v2:
time: 110 us
  Pallas kernels  109 us (99%)
    pallas_call x1, Pallas kernels, body(): pl.pallas_call(kernel, out_shape=pltpu.VMEM((1024, 256), BF), in_specs=[a...  109 us

profile of v2, /device:TPU:8, one launch (start us, length us, event | category | flops | bytes accessed | tf_op | source)
XLA Modules:
  0.0 109.8 jit_solution(716384663911402587)
XLA Ops:
  0.0 108.8 %hyena.1 = bf16[1024,256]{1,0:T(8,128)(2,1)S(1)} custom-call(bf16[1024,256]{1,0:T(8,128)(2,1)} %query.1, bf16[1024,256]{1,0:T(8,128)(2,1)} %key.1, bf16[1024,256]{1,0:T(8,128)(2,1)} %value.1, bf16[128,16,2,256]{3,2,1,0:T(2,128)(2,1)} %filt.1, bf16[256,8192]{1,0:T(8,128)(2,1)} %weight.1, bf16[3,512,512]{2,1,0:T(8,128)(2,1)} %constant.12.clone.moves, ...), custom_call_target="tpu_custom_call" | custom-call | tf_op jit(solution)/shard_map/hyena/pallas_call | solution.py:556
  108.8 1.0 copy.12

commit v3 on v2

--- a/solution.py
+++ b/solution.py
@@ -188,7 +188,6 @@
     ):
         pl.semaphore_signal(barrier, 1, device_id=peer, device_id_type=MESH)
 
-    pl.semaphore_wait(barrier, SEQ - 1 + 7)
 
     def weight_block(low, depth, which):
         at = pl.multiple_of(chan_of(low, depth, which) * 256, 256)
@@ -235,9 +234,6 @@
                 device_id={"chan": chan, "seq": y_hi * 4 + (x + peer) % 4},
                 device_id_type=MESH,
             ).start()
-
-    for step, seq_to in ((1, me), (7, far), (2, far), (6, me), (3, me), (5, far), (4, me), (0, far)):
-        send_weight_across(step, seq_to)
 
     local_done(0, 1, 2)
     for half in range(2):
@@ -280,8 +276,11 @@
         lax.fori_loop(1, SEQ, one, 0)
         pltpu.make_async_copy(send.at[me], recv.at[me], rs).start()
 
+    pl.semaphore_wait(barrier, SEQ - 1 + 7)
     for share in range(SHARES):
         spread(prod_send.at[share], prod_recv.at[share], prod_ss.at[share], prod_rs.at[share])
+    for step, seq_to in ((1, me), (7, far), (2, far), (6, me), (3, me), (5, far), (4, me), (0, far)):
+        send_weight_across(step, seq_to)
 
     local_start(5, 6, 7)
     local_done(4)
@@ -332,14 +331,6 @@
     lax.fori_loop(0, WAVES, rest_of_filter, 0)
     local_start(8, 9)
 
-    def near_weights(depth, carry):
-        send_weight_near(depth)
-        return carry
-
-    lax.fori_loop(0, 8, near_weights, 0)
-    arrive(weights.at[0], share_rs)
-    share_weight(1)
-    share_weight(7)
 
     local_done(5, 6, 7)
 
@@ -469,9 +460,17 @@
     local_done(9)
     inverse(0)
     inverse(1)
+
+    def late_weights(depth, carry):
+        send_weight_near(depth)
+        return carry
+
+    lax.fori_loop(0, 8, late_weights, 0)
+    arrive(weights.at[0], share_rs)
+    share_weight(1)
+    share_weight(7)
+
     gate(0)
-    share_weight(2)
-    share_weight(6)
 
     def pass_first(at, carry):
         pass_on(piece_of(at), 0)
@@ -479,7 +478,7 @@
 
     gate(1)
     lax.fori_loop(0, 2 * STREAMS, pass_first, 0)
-    for step in (3, 5, 4, 0):
+    for step in (2, 6, 3, 5, 4, 0):
         share_weight(step)
 
     def wait_weight(step):

time: 110 us -> 106 us (0.964)
  Pallas kernels: 109 us -> 105 us
    pallas_call x1, Pallas kernels: 109 us -> 105 us  [body(): pl.pallas_call(kernel, out_shape=pltpu.VMEM((1024, 256), BF), in_specs=[a...]
where the time goes in v3:
time: 106 us
  Pallas kernels  105 us (99%)
    pallas_call x1, Pallas kernels, body(): pl.pallas_call(kernel, out_shape=pltpu.VMEM((1024, 256), BF), in_specs=[a...  105 us

profile of v3, /device:TPU:8, one launch (start us, length us, event | category | flops | bytes accessed | tf_op | source)
XLA Modules:
  0.0 106.4 jit_solution(11918487766270564407)
XLA Ops:
  0.0 105.4 %hyena.1 = bf16[1024,256]{1,0:T(8,128)(2,1)S(1)} custom-call(bf16[1024,256]{1,0:T(8,128)(2,1)} %query.1, bf16[1024,256]{1,0:T(8,128)(2,1)} %key.1, bf16[1024,256]{1,0:T(8,128)(2,1)} %value.1, bf16[128,16,2,256]{3,2,1,0:T(2,128)(2,1)} %filt.1, bf16[256,8192]{1,0:T(8,128)(2,1)} %weight.1, bf16[3,512,512]{2,1,0:T(8,128)(2,1)} %constant.12.clone.moves, ...), custom_call_target="tpu_custom_call" | custom-call | tf_op jit(solution)/shard_map/hyena/pallas_call | solution.py:555
  105.4 1.0 copy.12

commit v4 on v3

--- a/solution.py
+++ b/solution.py
@@ -210,14 +210,14 @@
     row_across = pl.multiple_of((x % 2) * 128, 128)
     row_shared = pl.multiple_of(512 + x * 128, 128)
 
-    def send_weight_across(step, seq_to):
+    def send_weight_across(step, seq_to, late):
         depth = (z + step) % 8
         at = pl.multiple_of(chan_of(1 - y_lo, depth, core_across) * 256, 256)
         pltpu.make_async_remote_copy(
             weight.at[pl.ds(row_across, 128), pl.ds(at, 256)],
             weights.at[depth, pl.ds(row_shared, 128), :],
             weight_ss,
-            share_rs,
+            share_rs.at[late],
             device_id={"chan": chan_of(1 - y_lo, z, core_across), "seq": seq_to},
             device_id_type=MESH,
         ).start()
@@ -279,8 +279,8 @@
     pl.semaphore_wait(barrier, SEQ - 1 + 7)
     for share in range(SHARES):
         spread(prod_send.at[share], prod_recv.at[share], prod_ss.at[share], prod_rs.at[share])
-    for step, seq_to in ((1, me), (7, far), (2, far), (6, me), (3, me), (5, far), (4, me), (0, far)):
-        send_weight_across(step, seq_to)
+    for step, seq_to in ((1, me), (7, far), (2, far), (6, me)):
+        send_weight_across(step, seq_to, 0)
 
     local_start(5, 6, 7)
     local_done(4)
@@ -401,7 +401,7 @@
         return pl.ds(pl.multiple_of(piece * PIECE, PIECE), PIECE)
 
     def part(piece, slot, share):
-        return gated.at[rows_of(piece), pl.ds(slot * 256 + share * 128, 128)]
+        return gated.at[slot * SHARES + share, rows_of(piece), :]
 
     def gate_copy(kind, piece, share, source, target, device):
         return pltpu.make_async_remote_copy(
@@ -439,7 +439,7 @@
             rows = pl.ds(half * 512, 512)
             block = sorted_v[:, pl.ds(half * 32, 32), lanes].reshape(512, 128)
             conv = dot(moves_v[1], block)
-            gated[rows, lanes] = (query_v[rows, lanes].astype(F32) * conv).astype(BF)
+            gated[share, rows, :] = (query_v[rows, lanes].astype(F32) * conv).astype(BF)
 
         def send_gated(at, carry):
             piece = piece_of(at)
@@ -460,17 +460,16 @@
     local_done(9)
     inverse(0)
     inverse(1)
+    gate(0)
 
     def late_weights(depth, carry):
         send_weight_near(depth)
         return carry
 
     lax.fori_loop(0, 8, late_weights, 0)
-    arrive(weights.at[0], share_rs)
+    arrive(weights.at[0, pl.ds(0, 512), :], share_rs.at[0])
     share_weight(1)
     share_weight(7)
-
-    gate(0)
 
     def pass_first(at, carry):
         pass_on(piece_of(at), 0)
@@ -478,8 +477,10 @@
 
     gate(1)
     lax.fori_loop(0, 2 * STREAMS, pass_first, 0)
-    for step in (2, 6, 3, 5, 4, 0):
-        share_weight(step)
+    for step in (3, 5, 4, 0):
+        send_weight_across(step, far, 1)
+    share_weight(2)
+    share_weight(6)
 
     def wait_weight(step):
         depth = (z + step) % 8
@@ -487,7 +488,9 @@
 
     def term(piece, step):
         depth = (z + 7 - step) % 8 if piece // STREAMS == 0 else (z + 1 + step) % 8
-        return dot(gated[rows_of(piece), :], weights[depth])
+        rows = rows_of(piece)
+        values = jnp.concatenate([gated[at, rows, :] for at in range(4 * SHARES)], axis=1)
+        return dot(values, weights[depth])
 
     def ring_copy(piece, step):
         depth = z_up if piece // STREAMS == 0 else z_down
@@ -511,6 +514,10 @@
             ring_send[piece, 0] = term(piece, 0).astype(BF)
             ring_copy(piece, 0).start()
 
+    arrive(weights.at[0, pl.ds(0, 512), :], share_rs.at[1])
+    for step in (3, 5, 4, 0):
+        share_weight(step)
+
     def ring_step(step, carry):
         @pl.when(step < 4)
         def _():
@@ -542,7 +549,7 @@
         for wave in range(WAVES):
             arrive(filt_send.at[share, wave, pl.ds(0, SEQ - 1)], filt_ss.at[share, wave])
         for kind in range(3):
-            arrive(gated.at[:, pl.ds(0, 128)], gate_ss.at[kind, share])
+            arrive(gated.at[0], gate_ss.at[kind, share])
     arrive(weights.at[pl.ds(0, 6)], weight_ss)
     for piece in range(2 * STREAMS):
         arrive(ring_send.at[piece], ring_ss.at[piece])
@@ -578,7 +585,7 @@
             pltpu.VMEM((512, LANES), F32),
             pltpu.VMEM((SHARES, SEQ, 64, LANES), BF),
             pltpu.VMEM((SHARES, SEQ, 64, LANES), BF),
-            pltpu.VMEM((1024, 1024), BF),
+            pltpu.VMEM((4 * SHARES, 1024, 128), BF),
             pltpu.VMEM((8, 1024, 256), BF),
             pltpu.VMEM((2 * STREAMS, 7, PIECE, 256), BF),
             pltpu.VMEM((2 * STREAMS, 7, PIECE, 256), BF),
@@ -591,7 +598,7 @@
             dma((SHARES,)),
             dma,
             dma((8,)),
-            dma,
+            dma((2,)),
             dma((3, SHARES)),
             dma((3, SHARES, 2 * STREAMS)),
             dma((2 * STREAMS,)),

time: 106 us -> 105 us (level)
    pallas_call x1, Pallas kernels: 105 us -> 104 us  [body(): pl.pallas_call(kernel, out_shape=pltpu.VMEM((1024, 256), BF), in_specs=[a...]
where the time goes in v4:
time: 105 us
  Pallas kernels  104 us (99%)
    pallas_call x1, Pallas kernels, body(): pl.pallas_call(kernel, out_shape=pltpu.VMEM((1024, 256), BF), in_specs=[a...  104 us

profile of v4, /device:TPU:8, one launch (start us, length us, event | category | flops | bytes accessed | tf_op | source)
XLA Modules:
  0.0 104.9 jit_solution(13571079507113960434)
XLA Ops:
  0.0 103.9 %hyena.1 = bf16[1024,256]{1,0:T(8,128)(2,1)S(1)} custom-call(bf16[1024,256]{1,0:T(8,128)(2,1)} %query.1, bf16[1024,256]{1,0:T(8,128)(2,1)} %key.1, bf16[1024,256]{1,0:T(8,128)(2,1)} %value.1, bf16[128,16,2,256]{3,2,1,0:T(2,128)(2,1)} %filt.1, bf16[256,8192]{1,0:T(8,128)(2,1)} %weight.1, bf16[3,512,512]{2,1,0:T(8,128)(2,1)} %constant.12.clone.moves, ...), custom_call_target="tpu_custom_call" | custom-call | tf_op jit(solution)/shard_map/hyena/pallas_call | solution.py:562
  103.9 1.0 copy.12

commit v5 on v4

--- a/solution.py
+++ b/solution.py
@@ -279,7 +279,7 @@
     pl.semaphore_wait(barrier, SEQ - 1 + 7)
     for share in range(SHARES):
         spread(prod_send.at[share], prod_recv.at[share], prod_ss.at[share], prod_rs.at[share])
-    for step, seq_to in ((1, me), (7, far), (2, far), (6, me)):
+    for step, seq_to in ((1, me), (7, far)):
         send_weight_across(step, seq_to, 0)
 
     local_start(5, 6, 7)
@@ -461,13 +461,15 @@
     inverse(0)
     inverse(1)
     gate(0)
+    for step in (2, 6):
+        send_weight_across(step, far, 1)
 
     def late_weights(depth, carry):
         send_weight_near(depth)
         return carry
 
     lax.fori_loop(0, 8, late_weights, 0)
-    arrive(weights.at[0, pl.ds(0, 512), :], share_rs.at[0])
+    arrive(weights.at[0, pl.ds(0, 256), :], share_rs.at[0])
     share_weight(1)
     share_weight(7)
 
@@ -478,7 +480,8 @@
     gate(1)
     lax.fori_loop(0, 2 * STREAMS, pass_first, 0)
     for step in (3, 5, 4, 0):
-        send_weight_across(step, far, 1)
+        send_weight_across(step, far, 2)
+    arrive(weights.at[0, pl.ds(0, 256), :], share_rs.at[1])
     share_weight(2)
     share_weight(6)
 
@@ -514,7 +517,7 @@
             ring_send[piece, 0] = term(piece, 0).astype(BF)
             ring_copy(piece, 0).start()
 
-    arrive(weights.at[0, pl.ds(0, 512), :], share_rs.at[1])
+    arrive(weights.at[0, pl.ds(0, 512), :], share_rs.at[2])
     for step in (3, 5, 4, 0):
         share_weight(step)
 
@@ -598,7 +601,7 @@
             dma((SHARES,)),
             dma,
             dma((8,)),
-            dma((2,)),
+            dma((3,)),
             dma((3, SHARES)),
             dma((3, SHARES, 2 * STREAMS)),
             dma((2 * STREAMS,)),

time: 105 us -> 104 us (level)
  no operation moved by 1% of the time
where the time goes in v5:
time: 104 us
  Pallas kernels  103 us (99%)
    pallas_call x1, Pallas kernels, body(): pl.pallas_call(kernel, out_shape=pltpu.VMEM((1024, 256), BF), in_specs=[a...  103 us

profile of v5, /device:TPU:8, one launch (start us, length us, event | category | flops | bytes accessed | tf_op | source)
XLA Modules:
  0.0 103.9 jit_solution(6123938031055485051)
XLA Ops:
  0.0 102.9 %hyena.1 = bf16[1024,256]{1,0:T(8,128)(2,1)S(1)} custom-call(bf16[1024,256]{1,0:T(8,128)(2,1)} %query.1, bf16[1024,256]{1,0:T(8,128)(2,1)} %key.1, bf16[1024,256]{1,0:T(8,128)(2,1)} %value.1, bf16[128,16,2,256]{3,2,1,0:T(2,128)(2,1)} %filt.1, bf16[256,8192]{1,0:T(8,128)(2,1)} %weight.1, bf16[3,512,512]{2,1,0:T(8,128)(2,1)} %constant.12.clone.moves, ...), custom_call_target="tpu_custom_call" | custom-call | tf_op jit(solution)/shard_map/hyena/pallas_call | solution.py:565
  102.9 1.0 copy.12
